TPU v7x, 256 devices: a whole 4x4x8 slice. The times are simulated.
256 devices in a mesh: dp: 8 (over z), expert: 32 (over x, y, core).
Axes of the slice: x: 4, y: 4, z: 8, core: 2. Of those that a mesh axis runs over, the one named last changes fastest.
Arguments:
- tokens: bfloat16 [12288, 2048], P(('dp', 'expert')), may hold values from -6 to 6
- tokens_dot: bfloat16 [12288, 2048], P(('dp', 'expert')), may hold values from -6 to 6
- router: bfloat16 [2048, 64], replicated, may hold values from -0.125 to 0.125
- router_dot: bfloat16 [2048, 64], replicated, may hold values from -0.125 to 0.125
- expert_ids: int32 [12288, 8], P(('dp', 'expert')), may hold values from 0 to 63, all different within a row; in each aligned block of 48 rows (0 to 47, 48 to 95, ...) at most 12 rows name the same one
- priority: int32 [12288], P(('dp', 'expert')), may hold values from 0 to 12287, each once
- w_gate: bfloat16 [64, 768, 2048], P('expert', 'dp'), may hold values from -0.125 to 0.125
- w_up: bfloat16 [64, 768, 2048], P('expert', 'dp'), may hold values from -0.125 to 0.125
- w_down: bfloat16 [64, 768, 2048], P('expert', 'dp'), may hold values from -0.21875 to 0.21875
Outputs:
- mixed: bfloat16 [12288, 2048], P(('dp', 'expert'))
- mixed_dot: bfloat16 [12288, 2048], P(('dp', 'expert'))
Inputs may be any that keep to these rules, and one draw needn't show every extreme that they name: `expert_ids`: each token names 8 different experts; among the tokens of one device no expert is named more than 12 times, and exactly 12 times in some device. `priority`: each rank appears once.
All inputs are finite; a program needn't handle non-finite values.
Results may differ from a plain program's by a relative error of at most 0.0058.
Values may be sent and summed in bfloat16 or wider, within the bound.
A program may use at most 128 MiB of HBM per device.

v0:
```python
import jax
import jax.numpy as jnp
from jax import lax
from jax.sharding import PartitionSpec as P

TOP = 8
MOST = 12
CAP = 192


def hidden_units(stacked, gate_piece, up_piece):
    gate_all = jnp.einsum("ercd,efd->ercf", stacked, gate_piece, preferred_element_type=jnp.float32)
    up_all = jnp.einsum("ercd,efd->ercf", stacked, up_piece, preferred_element_type=jnp.float32)
    gate_p = gate_all[:, 0]
    up_p = up_all[:, 0]
    sigma = 1.0 / (1.0 + jnp.exp(-gate_p))
    act = gate_p * sigma * up_p
    act_dot = (
        sigma * (1.0 + gate_p * (1.0 - sigma)) * gate_all[:, 1] * up_p
        + gate_p * sigma * up_all[:, 1]
    )
    return jnp.stack([act, act_dot], axis=1).astype(jnp.bfloat16)


def shards(tokens, tokens_dot, router, router_dot, expert_ids, priority, w_gate, w_up, w_down):
    tok_count = tokens.shape[0]
    feat_width = tokens.shape[1]
    expert_count = router.shape[1]
    local_count = w_gate.shape[0]
    peer_count = lax.axis_size("expert")
    slot_count = MOST
    sentinel = 2**30
    member = (
        expert_ids[:, :, None] == jnp.arange(expert_count, dtype=jnp.int32)[None, None, :]
    ).astype(jnp.int32)
    member_flat = member.reshape(tok_count * TOP, expert_count)
    before = jnp.cumsum(member_flat, axis=0) - member_flat
    slot_index = jnp.sum(before * member_flat, axis=1)
    target = expert_ids.reshape(-1) * slot_count + slot_index
    owner_tok = jnp.arange(tok_count * TOP, dtype=jnp.int32) // TOP
    joined = jnp.concatenate([tokens, tokens_dot], axis=1)
    outgoing = (
        jnp.zeros((expert_count * slot_count, 2 * feat_width), jnp.bfloat16)
        .at[target]
        .set(joined[owner_tok])
    )
    out_ranks = (
        jnp.full((expert_count * slot_count,), sentinel, jnp.int32)
        .at[target]
        .set(priority[owner_tok])
    )
    outgoing = outgoing.reshape(peer_count, local_count * slot_count, 2 * feat_width)
    out_ranks = out_ranks.reshape(peer_count, local_count * slot_count)
    arrived, arrived_rank = (
        lax.all_to_all(outgoing, "expert", split_axis=0, concat_axis=0, tiled=True),
        lax.all_to_all(out_ranks, "expert", split_axis=0, concat_axis=0, tiled=True),
    )
    arrived = arrived.reshape(peer_count, local_count, slot_count, 2, feat_width)
    rank_local = jnp.transpose(
        arrived_rank.reshape(peer_count, local_count, slot_count), (1, 0, 2)
    ).reshape(local_count, peer_count * slot_count)
    usable = rank_local < sentinel
    ahead = jnp.sum(
        (usable[:, None, :] & (rank_local[:, None, :] < rank_local[:, :, None])).astype(jnp.int32),
        axis=2,
    )
    kept = usable & (ahead < CAP)
    placing = (
        kept[:, None, :] & (ahead[:, None, :] == jnp.arange(CAP, dtype=jnp.int32)[None, :, None])
    ).astype(jnp.bfloat16)
    placing = placing.reshape(local_count, CAP, peer_count, slot_count)
    packed = jnp.einsum(
        "ecsm,semrd->ercd", placing, arrived, preferred_element_type=jnp.float32
    ).astype(jnp.bfloat16)
    gate_piece = lax.all_gather(w_gate, "dp", axis=1, tiled=True)
    up_piece = lax.all_gather(w_up, "dp", axis=1, tiled=True)
    down_piece = lax.all_gather(w_down, "dp", axis=1, tiled=True)
    hidden = hidden_units(packed, gate_piece, up_piece)
    expert_out = jnp.einsum(
        "ercf,efd->ercd", hidden, down_piece, preferred_element_type=jnp.float32
    )
    out_bf = expert_out.astype(jnp.bfloat16)
    returning = jnp.einsum(
        "ecsm,ercd->semrd", placing, out_bf, preferred_element_type=jnp.float32
    ).astype(jnp.bfloat16)
    returning = returning.reshape(peer_count, local_count * slot_count, 2 * feat_width)
    landed = lax.all_to_all(returning, "expert", split_axis=0, concat_axis=0, tiled=True)
    landed = landed.reshape(expert_count * slot_count, 2, feat_width)
    results = landed[target].reshape(tok_count, TOP, 2, feat_width).astype(jnp.float32)
    logits = jnp.dot(tokens, router, preferred_element_type=jnp.float32)
    logits_dot = jnp.dot(tokens_dot, router, preferred_element_type=jnp.float32) + jnp.dot(
        tokens, router_dot, preferred_element_type=jnp.float32
    )
    member_f = member.astype(jnp.float32)
    chosen = jnp.sum(member_f * logits[:, None, :], axis=2)
    chosen_dot = jnp.sum(member_f * logits_dot[:, None, :], axis=2)
    expo = jnp.exp(chosen)
    gates = expo / jnp.sum(expo, axis=1, keepdims=True)
    gates_dot = gates * (chosen_dot - jnp.sum(gates * chosen_dot, axis=1, keepdims=True))
    mixed = jnp.sum(gates[:, :, None] * results[:, :, 0], axis=1)
    mixed_dot = jnp.sum(
        gates_dot[:, :, None] * results[:, :, 0] + gates[:, :, None] * results[:, :, 1], axis=1
    )
    return (mixed.astype(jnp.bfloat16), mixed_dot.astype(jnp.bfloat16))


def solution(mesh):
    return jax.shard_map(
        shards,
        mesh=mesh,
        in_specs=(
            P(("dp", "expert"), None),
            P(("dp", "expert"), None),
            P(),
            P(),
            P(("dp", "expert"), None),
            P(("dp", "expert")),
            P("expert", "dp", None),
            P("expert", "dp", None),
            P("expert", "dp", None),
        ),
        out_specs=(P(("dp", "expert"), None), P(("dp", "expert"), None)),
        check_vma=False,
    )
```

profile of v0, /device:TPU:8, one launch (start us, length us, event | category | flops | bytes accessed | tf_op | source)
XLA Modules:
  0.0 415.2 jit_solution(13426487562719504342)
XLA Ops:
  7.2 0.0 copy-start
  7.2 0.0 copy-start.2
  7.2 0.0 copy-start.1
  7.2 0.0 all-gather.4.cloned.1.call-start
  7.2 0.7 all-gather.4.cloned.1.call-update
  7.9 0.0 all-gather.6.cloned.1.call-start
  8.0 0.7 all-gather.6.cloned.1.call-update
  8.7 0.0 all-gather.8.cloned.1.call-start
  8.7 0.7 all-gather.8.cloned.1.call-update
  9.4 0.8 copy.37
  10.2 0.1 eq.53
  10.3 0.1 eq.49
  10.4 0.9 reduce-window.6
  11.3 0.2 slice_reduce_fusion
  11.6 0.7 broadcast_multiply_fusion
  12.3 0.1 copy.38
  12.3 0.1 mul.102
  12.5 0.1 fusion.38
  12.6 1.7 fusion.48
  14.3 2.1 fusion.46
  16.4 2.1 fusion.47
  18.5 30.2 %select_select_fusion = s32[384]{0:T(512)S(1)} fusion(s32[384]{0:T(512)S(1)} %fusion.43, s32[]{:T(128)} %bitcast.2, s32[]{:T(128)} %bitcast.3, s32[]{:T(128)} %bitcast.4, s32[]{:T(128)} %bitcast.5, s32[]{:T(128)} %bitcast.6, s32[]{:T(128)} %bitcast.7, s32[]{:T(128)} %bitcast.8, s32[]{:T(128)} %bitcast.9, s32[]{:T(128)} %bitcast.10, s32[]{:T(128)} %bitcast.11, ...), kind=kLoop, calls=%fused_computation.72 | loop fusion | flops 36096 | bytes 3264 | tf_op jit(solution)/shard_map/gather | solution.py:50
  48.7 2.9 scatter_custom_fusion.1
  51.6 0.7 all_to_all.13
  52.3 8.2 %all-to-all-start.1 = ((s32[32,1,24]{2,1,0:T(1,128)}), s32[32,1,24]{2,1,0:T(1,128)S(1)}, u32[]{:S(2)}, u32[]{:S(2)}) async-start(s32[32,1,24]{2,1,0:T(1,128)} %bitcast.50), calls=%async_computation.1 | async-start | bytes 32768 | tf_op jit(solution)/shard_map/all_to_all | solution.py:56
  60.5 0.0 copy-done.2
  60.5 0.0 copy-done.1
  60.5 17.9 %scatter_custom_fusion = bf16[768,4096]{1,0:T(8,128)(2,1)} fusion(s32[384]{0:T(512)S(1)} %fusion.42, bf16[48,4096]{1,0:T(8,128)(2,1)S(1)} %pad_maximum_fusion, s32[1024]{0:T(1024)S(1)} %pad_clamp_fusion.1, bf16[]{:T(256)} %constant.15.clone.1), kind=kCustom, calls=%fused_computation.22 | custom fusion | bytes 6291458 | tf_op jit(solution)/shard_map/scatter | solution.py:45
  78.4 0.0 all-to-all-done.1
  78.4 7.4 %all-to-all-start = ((bf16[32,24,4096]{2,1,0:T(8,128)(2,1)}), bf16[32,24,4096]{2,1,0:T(8,128)(2,1)}, u32[]{:S(2)}, u32[]{:S(2)}) async-start(bf16[32,24,4096]{2,1,0:T(8,128)(2,1)} %bitcast.133), calls=%async_computation | async-start | bytes 12582912 | tf_op jit(solution)/shard_map/all_to_all | solution.py:55
  85.8 0.1 copy.43
  85.9 0.1 copy.44
  86.0 0.1 reshape.198
  86.1 0.3 convert_reduce_fusion
  86.5 0.1 reduce_sum.81
  86.6 0.1 copy.45
  86.7 86.7 %all-to-all-done = bf16[32,24,4096]{2,1,0:T(8,128)(2,1)} async-done(((bf16[32,24,4096]{2,1,0:T(8,128)(2,1)}), bf16[32,24,4096]{2,1,0:T(8,128)(2,1)}, u32[]{:S(2)}, u32[]{:S(2)}) %all-to-all-start) | async-done | bytes 6291488 | tf_op jit(solution)/shard_map/all_to_all | solution.py:55
  173.4 11.5 %reshape.196 = bf16[32,2,12,2,2048]{4,3,2,1,0:T(2,128)(2,1)} reshape(bf16[32,24,4096]{2,1,0:T(8,128)(2,1)} %all-to-all-done) | data formatting | bytes 12582912 | tf_op jit(solution)/shard_map/reshape | solution.py:58
  184.9 8.9 %bitcast_convert_fusion = bf16[2,2,2048,192]{2,3,1,0:T(8,128)(2,1)} fusion(bf16[32,2,12,2,2048]{4,3,2,1,0:T(2,128)(2,1)} %reshape.196, s32[2,32,12]{1,2,0:T(8,128)S(1)} %copy.45, pred[2,32,12]{1,2,0:T(8,128)(4,1)S(1)} %compare_and_fusion), kind=kOutput, calls=%fused_computation.10 | convolution fusion | flops 1209827328 | bytes 9441024 | tf_op jit(solution)/shard_map/ecsm,semrd->ercd/dot_general | solution.py:72
  193.8 0.0 all-gather.4.cloned.1.call-done
  193.8 6.4 %fusion.4 = f32[2,2,192,768]{3,2,1,0:T(8,128)S(1)} fusion(bf16[2,768,2048]{2,1,0:T(8,128)(2,1)} %all-gather.4.cloned.1.call-done, bf16[2,2,2048,192]{2,3,1,0:T(8,128)(2,1)} %bitcast_convert_fusion), kind=kOutput, calls=%fused_computation.8 | convolution fusion | flops 2415919104 | bytes 11796480 | tf_op jit(solution)/shard_map/ercd,efd->ercf/dot_general | solution.py:12
  200.2 0.0 all-gather.6.cloned.1.call-done
  200.3 6.4 %fusion.2 = f32[2,2,192,768]{3,2,1,0:T(8,128)S(1)} fusion(bf16[2,768,2048]{2,1,0:T(8,128)(2,1)} %all-gather.6.cloned.1.call-done, bf16[2,2,2048,192]{2,3,1,0:T(8,128)(2,1)} %bitcast_convert_fusion), kind=kOutput, calls=%fused_computation.6 | convolution fusion | flops 2415919104 | bytes 11796480 | tf_op jit(solution)/shard_map/ercd,efd->ercf/dot_general | solution.py:13
  206.7 1.7 multiply_convert_fusion
  208.4 28.7 %all-gather.8.cloned.1.call-done = bf16[2,768,2048]{2,1,0:T(8,128)(2,1)} async-done(((bf16[2,96,2048]{2,1,0:T(8,128)(2,1)}), bf16[2,768,2048]{2,1,0:T(8,128)(2,1)}) %all-gather.8.cloned.1.call-update) | async-done | bytes 6291472 | tf_op jit(solution)/shard_map/all_gather | solution.py:77
  237.1 5.8 %fusion.10 = bf16[2,2,192,2048]{3,2,1,0:T(8,128)(2,1)S(1)} fusion(bf16[2,768,2048]{2,1,0:T(8,128)(2,1)} %all-gather.8.cloned.1.call-done, bf16[2,1,192,768]{3,2,1,0:T(8,128)(2,1)} %get-tuple-element.9, bf16[2,1,192,768]{3,2,1,0:T(8,128)(2,1)} %get-tuple-element.8), kind=kOutput, calls=%fused_computation.14 | convolution fusion | flops 2418081792 | bytes 10616832 | tf_op jit(solution)/shard_map/ercf,efd->ercd/dot_general | solution.py:79
  242.8 2.5 convert_bitcast_fusion
  245.4 14.0 %copy.48 = bf16[32,2,12,2,2048]{4,3,2,1,0:T(2,128)(2,1)} copy(bf16[32,2,12,2,2048]{4,0,2,3,1:T(8,128)(2,1)S(1)} %convert_bitcast_fusion) | data formatting | bytes 12582912 | tf_op jit(solution)/shard_map/convert_element_type | solution.py:85
  259.4 11.1 %reshape.199 = bf16[32,24,4096]{2,1,0:T(8,128)(2,1)} reshape(bf16[32,2,12,2,2048]{4,3,2,1,0:T(2,128)(2,1)} %copy.48) | data formatting | bytes 12582912 | tf_op jit(solution)/shard_map/reshape | solution.py:86
  270.5 7.6 %all-to-all-start.2 = ((bf16[32,24,4096]{2,1,0:T(8,128)(2,1)}), bf16[32,24,4096]{2,1,0:T(8,128)(2,1)}, u32[]{:S(2)}, u32[]{:S(2)}) async-start(bf16[32,24,4096]{2,1,0:T(8,128)(2,1)} %reshape.199), calls=%async_computation.2 | async-start | bytes 12582912 | tf_op jit(solution)/shard_map/all_to_all | solution.py:87
  278.1 0.0 copy-done
  278.1 0.2 fusion.50
  278.3 0.2 fusion.49
  278.5 0.0 copy-done.3
  278.5 0.2 convolution_add_fusion
  278.7 0.2 multiply_reduce_fusion.1
  279.0 0.1 exponential_reduce_fusion
  279.1 0.2 multiply_reduce_fusion.3
  279.3 0.1 subtract_multiply_fusion
  279.4 86.3 %all-to-all-done.2 = bf16[32,24,4096]{2,1,0:T(8,128)(2,1)} async-done(((bf16[32,24,4096]{2,1,0:T(8,128)(2,1)}), bf16[32,24,4096]{2,1,0:T(8,128)(2,1)}, u32[]{:S(2)}, u32[]{:S(2)}) %all-to-all-start.2) | async-done | bytes 6291488 | tf_op jit(solution)/shard_map/all_to_all | solution.py:87
  365.6 11.1 %reshape.200 = bf16[768,2,2048]{2,1,0:T(2,128)(2,1)} reshape(bf16[32,24,4096]{2,1,0:T(8,128)(2,1)} %all-to-all-done.2) | data formatting | bytes 12582912 | tf_op jit(solution)/shard_map/reshape | solution.py:88
  376.8 17.7 %gather_fusion = bf16[384,2,2048]{2,1,0:T(2,128)(2,1)S(1)} fusion(bf16[768,2,2048]{2,1,0:T(2,128)(2,1)} %reshape.200, s32[1024]{0:T(1024)S(1)} %pad_clamp_fusion), kind=kCustom, calls=%fused_computation.1 | custom fusion | bytes 6292992 | tf_op jit(solution)/shard_map/gather | solution.py:89
  394.5 6.5 %fusion.45 = (f32[48,8,1,2048]{3,2,1,0:T(1,128)S(1)}, f32[48,8,1,2048]{3,2,1,0:T(1,128)}) fusion(bf16[48,8,2,2048]{3,2,1,0:T(2,128)(2,1)S(1)} %bitcast.132), kind=kLoop, calls=%fused_computation.80 | loop fusion | bytes 12582912 | tf_op jit(solution)/shard_map/slice | solution.py:100
  401.0 7.5 %fusion.14 = (bf16[48,2048]{1,0:T(8,128)(2,1)}, bf16[48,2048]{1,0:T(8,128)(2,1)}) fusion(f32[48,8,1,2048]{3,2,1,0:T(1,128)} %get-tuple-element.11, f32[48,8,1,2048]{3,2,1,0:T(1,128)S(1)} %get-tuple-element.10, f32[48,8]{1,0:T(8,128)S(1)} %subtract_multiply_fusion, f32[48,8]{1,0:T(8,128)S(1)} %get-tuple-element.7), kind=kLoop, calls=%fused_computation.18 | loop fusion | flops 4521984 | bytes 6687744 | tf_op jit(solution)/shard_map/reduce_sum | solution.py:101
  (11 shorter events, 0.2 us)
Async XLA Ops:
  7.2 270.9 %copy-start = (bf16[2048,64]{0,1:T(8,128)(2,1)S(1)}, bf16[2048,64]{0,1:T(8,128)(2,1)}, u32[]{:S(2)}) copy-start(bf16[2048,64]{0,1:T(8,128)(2,1)} %param.11) | copy-start | bytes 786436
  7.2 53.3 %copy-start.2 = (bf16[48,2048]{1,0:T(8,128)(2,1)S(1)}, bf16[48,2048]{1,0:T(8,128)(2,1)}, u32[]{:S(2)}) copy-start(bf16[48,2048]{1,0:T(8,128)(2,1)} %param.10) | copy-start | bytes 589828
  7.2 53.3 %copy-start.1 = (bf16[48,2048]{1,0:T(8,128)(2,1)S(1)}, bf16[48,2048]{1,0:T(8,128)(2,1)}, u32[]{:S(2)}) copy-start(bf16[48,2048]{1,0:T(8,128)(2,1)} %param.9) | copy-start | bytes 589828
  7.2 186.6 %all-gather.4.cloned.1.call-start = ((), (), s32[]{:S(2)}) async-start(), calls=%async_computation.3 | async-start | bytes 7077888 | tf_op jit(solution)/shard_map/all_gather | solution.py:75
  7.9 192.3 %all-gather.6.cloned.1.call-start = ((), (), s32[]{:S(2)}) async-start(), calls=%async_computation.4 | async-start | bytes 7077888 | tf_op jit(solution)/shard_map/all_gather | solution.py:76
  8.7 228.4 %all-gather.8.cloned.1.call-start = ((), (), s32[]{:S(2)}) async-start(), calls=%async_computation.5 | async-start | bytes 7077888 | tf_op jit(solution)/shard_map/all_gather | solution.py:77
  52.3 26.1 %all-to-all-start.1 = ((s32[32,1,24]{2,1,0:T(1,128)}), s32[32,1,24]{2,1,0:T(1,128)S(1)}, u32[]{:S(2)}, u32[]{:S(2)}) async-start(s32[32,1,24]{2,1,0:T(1,128)} %bitcast.50), calls=%async_computation.1 | async-start | bytes 32768 | tf_op jit(solution)/shard_map/all_to_all | solution.py:56
  78.4 95.0 %all-to-all-start = ((bf16[32,24,4096]{2,1,0:T(8,128)(2,1)}), bf16[32,24,4096]{2,1,0:T(8,128)(2,1)}, u32[]{:S(2)}, u32[]{:S(2)}) async-start(bf16[32,24,4096]{2,1,0:T(8,128)(2,1)} %bitcast.133), calls=%async_computation | async-start | bytes 12582912 | tf_op jit(solution)/shard_map/all_to_all | solution.py:55
  270.5 8.0 %copy-start.3 = (bf16[2048,64]{0,1:T(8,128)(2,1)S(1)}, bf16[2048,64]{0,1:T(8,128)(2,1)}, u32[]{:S(2)}) copy-start(bf16[2048,64]{0,1:T(8,128)(2,1)} %param.12) | copy-start | bytes 786436
  270.5 95.2 %all-to-all-start.2 = ((bf16[32,24,4096]{2,1,0:T(8,128)(2,1)}), bf16[32,24,4096]{2,1,0:T(8,128)(2,1)}, u32[]{:S(2)}, u32[]{:S(2)}) async-start(bf16[32,24,4096]{2,1,0:T(8,128)(2,1)} %reshape.199), calls=%async_computation.2 | async-start | bytes 12582912 | tf_op jit(solution)/shard_map/all_to_all | solution.py:87
Sparse Core Ops, SparseCore 0:
  9.8 77.3 all-gather.3
  89.0 73.0 all-gather.5
  163.9 73.0 all-gather.7
where the time goes:
time: 420 us; the launch traced here: 415 us
  waiting for transfers between devices  204 us (49%)
  local copies, waits for them, and re-layouts  101 us (24%)
  other arithmetic  42.2 us (10%)
  matrix products  30.7 us (7%)
  starting transfers between devices  23.3 us (6%)
  between operations  14.2 us (3%)
    all_to_all x1, waiting for transfers between devices, shards(): lax.all_to_all(outgoing, 'expert', split_axis=0, concat_axis=0, tiled=True)  86.7 us
    all_to_all x1, waiting for transfers between devices, shards(): lax.all_to_all(returning, 'expert', split_axis=0, concat_axis=0, tiled=True)  86.3 us
    gather x1, other arithmetic, shards(): priority[owner_tok]  30.2 us
    all_gather x1, waiting for transfers between devices, shards(): down_piece = lax.all_gather(w_down, 'dp', axis=1, tiled=True)  28.7 us
    scatter x1, local copies, waits for them, and re-layouts, shards(): outgoing = jnp.zeros((expert_count * slot_count, 2 * feat_width), jnp.bfl...  17.9 us
    gather x1, local copies, waits for them, and re-layouts, shards(): landed[target].reshape(tok_count, TOP, 2, feat_width).astype(jnp.float32)  17.7 us
    convert_element_type x1, local copies, waits for them, and re-layouts, shards(): returning = jnp.einsum('ecsm,ercd->semrd', placing, out_bf, preferred_ele...  14 us
    reshape x1, local copies, waits for them, and re-layouts, shards(): arrived.reshape(peer_count, local_count, slot_count, 2, feat_width)  11.5 us
  transfers between devices with their start and end apart: 6, of which 3 were waited for; matrix products, arithmetic and copies ran while one was open for 23% of the time, Pallas kernels for 0%

commit v1 on v0

--- a/solution.py
+++ b/solution.py
@@ -74,7 +74,9 @@
     ).astype(jnp.bfloat16)
     gate_piece = lax.all_gather(w_gate, "dp", axis=1, tiled=True)
     up_piece = lax.all_gather(w_up, "dp", axis=1, tiled=True)
-    down_piece = lax.all_gather(w_down, "dp", axis=1, tiled=True)
+    down_piece = jnp.concatenate(
+        jax.lax.all_to_all(jnp.stack([w_down] * jax.lax.axis_size("dp")), "dp", 0, 0), axis=1
+    )
     hidden = hidden_units(packed, gate_piece, up_piece)
     expert_out = jnp.einsum(
         "ercf,efd->ercd", hidden, down_piece, preferred_element_type=jnp.float32

time: 420 us -> 512 us (1.22)
  waiting for transfers between devices: 204 us -> 281 us
  local copies, waits for them, and re-layouts: 101 us -> 109 us
  starting transfers between devices: 23.3 us -> 29.6 us
    all_to_all x0 -> x1, waiting for transfers between devices: none -> 106 us  [shards(): jax.lax.all_to_all(jnp.stack([w_down] * jax.lax.axis_size('dp')), 'dp', 0...]
    all_gather x1 -> x0, waiting for transfers between devices: 28.7 us -> none  [shards(): down_piece = lax.all_gather(w_down, 'dp', axis=1, tiled=True)]
    all_to_all x0 -> x1, starting transfers between devices: none -> 8.73 us  [shards(): jax.lax.all_to_all(jnp.stack([w_down] * jax.lax.axis_size('dp')), 'dp', 0...]
    all_to_all x0 -> x1, local copies, waits for them, and re-layouts: none -> 6.57 us  [shards(): jax.lax.all_to_all(jnp.stack([w_down] * jax.lax.axis_size('dp')), 'dp', 0...]
    dot_general x1, matrix products: 2.52 us -> 8.34 us  [shards(): jnp.einsum('ecsm,ercd->semrd', placing, out_bf, preferred_element_type=jn...]
    dot_general x1 -> x0, matrix products: 5.77 us -> none  [shards(): jnp.einsum('ercf,efd->ercd', hidden, down_piece, preferred_element_type=j...]
  transfers between devices with their start and end apart: 6 -> 6, of which waited for: 3 -> 3; matrix products, arithmetic and copies ran while one was open for 23% -> 20% of each run, Pallas kernels for 0% -> 0%
where the time goes in v1:
time: 512 us; the launch traced here: 507 us
  waiting for transfers between devices  281 us (55%)
  local copies, waits for them, and re-layouts  109 us (21%)
  other arithmetic  42.8 us (8%)
  matrix products  30.6 us (6%)
  starting transfers between devices  29.6 us (6%)
  between operations  14.5 us (3%)
    all_to_all x1, waiting for transfers between devices, shards(): jax.lax.all_to_all(jnp.stack([w_down] * jax.lax.axis_size('dp')), 'dp', 0...  106 us
    all_to_all x1, waiting for transfers between devices, shards(): lax.all_to_all(outgoing, 'expert', split_axis=0, concat_axis=0, tiled=True)  86.8 us
    all_to_all x1, waiting for transfers between devices, shards(): lax.all_to_all(returning, 'expert', split_axis=0, concat_axis=0, tiled=True)  86.2 us
    gather x1, other arithmetic, shards(): priority[owner_tok]  30 us
    scatter x1, local copies, waits for them, and re-layouts, shards(): outgoing = jnp.zeros((expert_count * slot_count, 2 * feat_width), jnp.bfl...  17.8 us
    gather x1, local copies, waits for them, and re-layouts, shards(): landed[target].reshape(tok_count, TOP, 2, feat_width).astype(jnp.float32)  17.7 us
    convert_element_type x1, local copies, waits for them, and re-layouts, shards(): returning = jnp.einsum('ecsm,ercd->semrd', placing, out_bf, preferred_ele...  12.7 us
    reshape x1, local copies, waits for them, and re-layouts, shards(): arrived.reshape(peer_count, local_count, slot_count, 2, feat_width)  11.2 us
  transfers between devices with their start and end apart: 6, of which 3 were waited for; matrix products, arithmetic and copies ran while one was open for 20% of the time, Pallas kernels for 0%

profile of v1, /device:TPU:8, one launch (start us, length us, event | category | flops | bytes accessed | tf_op | source)
XLA Modules:
  0.0 507.5 jit_solution(11513106082147393432)
XLA Ops:
  7.2 0.0 copy-start
  7.2 0.0 all-gather.5.cloned.1.call-start
  7.2 0.7 all-gather.5.cloned.1.call-update
  7.9 0.8 copy.38
  8.7 0.1 eq.53
  8.8 0.1 eq.49
  8.9 0.9 reduce-window.6
  9.8 0.2 slice_reduce_fusion
  10.1 0.7 broadcast_multiply_fusion
  10.8 0.1 copy.39
  10.8 0.1 mul.102
  11.0 0.1 fusion.36
  11.1 1.7 fusion.47
  12.8 2.1 fusion.45
  14.9 2.1 fusion.46
  16.9 30.0 %select_select_fusion = s32[384]{0:T(512)S(1)} fusion(s32[384]{0:T(512)S(1)} %fusion.41, s32[]{:T(128)} %bitcast.2, s32[]{:T(128)} %bitcast.3, s32[]{:T(128)} %bitcast.4, s32[]{:T(128)} %bitcast.5, s32[]{:T(128)} %bitcast.6, s32[]{:T(128)} %bitcast.7, s32[]{:T(128)} %bitcast.8, s32[]{:T(128)} %bitcast.9, s32[]{:T(128)} %bitcast.10, s32[]{:T(128)} %bitcast.11, ...), kind=kLoop, calls=%fused_computation.70 | loop fusion | flops 36096 | bytes 3264 | tf_op jit(solution)/shard_map/gather | solution.py:50
  46.9 2.9 scatter_custom_fusion.1
  49.9 0.7 all_to_all.16
  50.5 8.2 %all-to-all-start.1 = ((s32[32,1,24]{2,1,0:T(1,128)}), s32[32,1,24]{2,1,0:T(1,128)S(1)}, u32[]{:S(2)}, u32[]{:S(2)}) async-start(s32[32,1,24]{2,1,0:T(1,128)} %bitcast.50), calls=%async_computation.1 | async-start | bytes 32768 | tf_op jit(solution)/shard_map/all_to_all | solution.py:56
  58.7 1.1 pad_maximum_fusion
  59.8 17.8 %scatter_custom_fusion = bf16[768,4096]{1,0:T(8,128)(2,1)} fusion(s32[384]{0:T(512)S(1)} %fusion.40, bf16[48,4096]{1,0:T(8,128)(2,1)S(1)} %pad_maximum_fusion, s32[1024]{0:T(1024)S(1)} %pad_clamp_fusion.1, bf16[]{:T(256)} %constant.15.clone.1), kind=kCustom, calls=%fused_computation.20 | custom fusion | bytes 6291458 | tf_op jit(solution)/shard_map/scatter | solution.py:45
  77.6 0.0 all-to-all-done.1
  77.6 7.6 %all-to-all-start = ((bf16[32,24,4096]{2,1,0:T(8,128)(2,1)}), bf16[32,24,4096]{2,1,0:T(8,128)(2,1)}, u32[]{:S(2)}, u32[]{:S(2)}) async-start(bf16[32,24,4096]{2,1,0:T(8,128)(2,1)} %bitcast.134), calls=%async_computation | async-start | bytes 12582912 | tf_op jit(solution)/shard_map/all_to_all | solution.py:55
  85.2 0.0 all-gather.3.cloned.1.call-start
  85.2 0.7 all-gather.3.cloned.1.call-update
  85.9 86.8 %all-to-all-done = bf16[32,24,4096]{2,1,0:T(8,128)(2,1)} async-done(((bf16[32,24,4096]{2,1,0:T(8,128)(2,1)}), bf16[32,24,4096]{2,1,0:T(8,128)(2,1)}, u32[]{:S(2)}, u32[]{:S(2)}) %all-to-all-start) | async-done | bytes 6291488 | tf_op jit(solution)/shard_map/all_to_all | solution.py:55
  172.8 0.0 copy-done.2
  172.8 3.4 stack.6
  176.2 8.7 %all-to-all-start.2 = ((bf16[8,2,96,2048]{3,2,1,0:T(8,128)(2,1)}), bf16[8,2,96,2048]{3,2,1,0:T(8,128)(2,1)}, u32[]{:S(2)}, u32[]{:S(2)}) async-start(bf16[8,2,96,2048]{3,2,1,0:T(8,128)(2,1)} %stack.6), calls=%async_computation.2 | async-start | bytes 12582912 | tf_op jit(solution)/shard_map/all_to_all | solution.py:78
  184.9 0.1 copy.44
  185.0 0.1 copy.45
  185.1 0.1 reshape.206
  185.2 0.3 convert_reduce_fusion
  185.5 0.1 reduce_sum.81
  185.6 0.1 copy.46
  185.7 11.2 %reshape.204 = bf16[32,2,12,2,2048]{4,3,2,1,0:T(2,128)(2,1)} reshape(bf16[32,24,4096]{2,1,0:T(8,128)(2,1)} %all-to-all-done) | data formatting | bytes 12582912 | tf_op jit(solution)/shard_map/reshape | solution.py:58
  196.9 8.9 %bitcast_convert_fusion = bf16[2,2,2048,192]{2,3,1,0:T(8,128)(2,1)} fusion(bf16[32,2,12,2,2048]{4,3,2,1,0:T(2,128)(2,1)} %reshape.204, s32[2,32,12]{1,2,0:T(8,128)S(1)} %copy.46, pred[2,32,12]{1,2,0:T(8,128)(4,1)S(1)} %compare_and_fusion), kind=kOutput, calls=%fused_computation.8 | convolution fusion | flops 1209827328 | bytes 9441024 | tf_op jit(solution)/shard_map/ecsm,semrd->ercd/dot_general | solution.py:72
  205.8 6.4 %fusion = f32[2,2,192,768]{3,2,1,0:T(8,128)S(1)} fusion(bf16[2,768,2048]{2,1,0:T(8,128)(2,1)} %all-gather.5.cloned.1.call-done, bf16[2,2,2048,192]{2,3,1,0:T(8,128)(2,1)} %bitcast_convert_fusion), kind=kOutput, calls=%fused_computation.4 | convolution fusion | flops 2415919104 | bytes 11796480 | tf_op jit(solution)/shard_map/ercd,efd->ercf/dot_general | solution.py:13
  212.2 0.0 all-gather.3.cloned.1.call-done
  212.2 6.4 %fusion.2 = f32[2,2,192,768]{3,2,1,0:T(8,128)S(1)} fusion(bf16[2,768,2048]{2,1,0:T(8,128)(2,1)} %all-gather.3.cloned.1.call-done, bf16[2,2,2048,192]{2,3,1,0:T(8,128)(2,1)} %bitcast_convert_fusion), kind=kOutput, calls=%fused_computation.6 | convolution fusion | flops 2415919104 | bytes 11796480 | tf_op jit(solution)/shard_map/ercd,efd->ercf/dot_general | solution.py:12
  218.6 1.5 multiply_convert_fusion
  220.1 106.1 %all-to-all-done.2 = bf16[8,2,96,2048]{3,2,1,0:T(8,128)(2,1)} async-done(((bf16[8,2,96,2048]{3,2,1,0:T(8,128)(2,1)}), bf16[8,2,96,2048]{3,2,1,0:T(8,128)(2,1)}, u32[]{:S(2)}, u32[]{:S(2)}) %all-to-all-start.2) | async-done | bytes 6291488 | tf_op jit(solution)/shard_map/all_to_all | solution.py:78
  326.2 6.6 %copy.49 = bf16[8,2,96,2048]{3,2,0,1:T(8,128)(2,1)} copy(bf16[8,2,96,2048]{3,2,1,0:T(8,128)(2,1)} %all-to-all-done.2) | data formatting | bytes 12582912 | tf_op jit(solution)/shard_map/all_to_all | solution.py:78
  332.7 0.0 copy-done.4
  332.7 8.3 %convert_bitcast_fusion = bf16[32,2,12,2,2048]{4,0,2,3,1:T(8,128)(2,1)} fusion(bf16[2,768,2048,1]{2,1,3,0:T(8,128)(2,1)} %bitcast.135, bf16[2,1,192,768]{3,2,1,0:T(8,128)(2,1)S(1)} %copy-done.4, bf16[2,1,192,768]{3,2,1,0:T(8,128)(2,1)S(1)} %get-tuple-element.8, s32[2,32,12]{1,2,0:T(8,128)S(1)} %copy.46, pred[2,32,12]{1,2,0:T(8,128)(4,1)S(1)} %compare_and_fusion), kind=kOutput, calls=%fused_computation.11 | convolution fusion | flops 3629481984 | bytes 13766400 | tf_op jit(solution)/shard_map/ecsm,ercd->semrd/dot_general | solution.py:85
  341.1 12.7 %copy.50 = bf16[32,2,12,2,2048]{4,3,2,1,0:T(2,128)(2,1)} copy(bf16[32,2,12,2,2048]{4,0,2,3,1:T(8,128)(2,1)} %convert_bitcast_fusion) | data formatting | bytes 12582912 | tf_op jit(solution)/shard_map/convert_element_type | solution.py:87
  353.8 11.1 %reshape.209 = bf16[32,24,4096]{2,1,0:T(8,128)(2,1)} reshape(bf16[32,2,12,2,2048]{4,3,2,1,0:T(2,128)(2,1)} %copy.50) | data formatting | bytes 12582912 | tf_op jit(solution)/shard_map/reshape | solution.py:88
  364.9 5.1 %all-to-all-start.3 = ((bf16[32,24,4096]{2,1,0:T(8,128)(2,1)}), bf16[32,24,4096]{2,1,0:T(8,128)(2,1)}, u32[]{:S(2)}, u32[]{:S(2)}) async-start(bf16[32,24,4096]{2,1,0:T(8,128)(2,1)} %reshape.209), calls=%async_computation.3 | async-start | bytes 12582912 | tf_op jit(solution)/shard_map/all_to_all | solution.py:89
  370.0 0.0 copy-done
  370.0 0.0 copy-done.3
  370.0 0.2 fusion.49
  370.2 0.0 copy-done.1
  370.3 0.2 fusion.48
  370.5 0.0 copy-done.5
  370.5 0.2 convolution_add_fusion
  370.7 0.2 multiply_reduce_fusion.1
  371.0 0.1 exponential_reduce_fusion
  371.1 0.2 multiply_reduce_fusion.3
  371.3 0.1 subtract_multiply_fusion
  371.3 86.2 %all-to-all-done.3 = bf16[32,24,4096]{2,1,0:T(8,128)(2,1)} async-done(((bf16[32,24,4096]{2,1,0:T(8,128)(2,1)}), bf16[32,24,4096]{2,1,0:T(8,128)(2,1)}, u32[]{:S(2)}, u32[]{:S(2)}) %all-to-all-start.3) | async-done | bytes 6291488 | tf_op jit(solution)/shard_map/all_to_all | solution.py:89
  457.6 11.1 %reshape.210 = bf16[768,2,2048]{2,1,0:T(2,128)(2,1)} reshape(bf16[32,24,4096]{2,1,0:T(8,128)(2,1)} %all-to-all-done.3) | data formatting | bytes 12582912 | tf_op jit(solution)/shard_map/reshape | solution.py:90
  468.7 17.7 %gather_fusion = bf16[384,2,2048]{2,1,0:T(2,128)(2,1)S(1)} fusion(bf16[768,2,2048]{2,1,0:T(2,128)(2,1)} %reshape.210, s32[1024]{0:T(1024)S(1)} %pad_clamp_fusion), kind=kCustom, calls=%fused_computation.1 | custom fusion | bytes 6292992 | tf_op jit(solution)/shard_map/gather | solution.py:91
  486.4 6.5 %fusion.44 = (f32[48,8,1,2048]{3,2,1,0:T(1,128)S(1)}, f32[48,8,1,2048]{3,2,1,0:T(1,128)}) fusion(bf16[48,8,2,2048]{3,2,1,0:T(2,128)(2,1)S(1)} %bitcast.133), kind=kLoop, calls=%fused_computation.78 | loop fusion | bytes 12582912 | tf_op jit(solution)/shard_map/slice | solution.py:102
  492.9 7.5 %fusion.9 = (bf16[48,2048]{1,0:T(8,128)(2,1)}, bf16[48,2048]{1,0:T(8,128)(2,1)}) fusion(f32[48,8,1,2048]{3,2,1,0:T(1,128)} %get-tuple-element.11, f32[48,8,1,2048]{3,2,1,0:T(1,128)S(1)} %get-tuple-element.10, f32[48,8]{1,0:T(8,128)S(1)} %subtract_multiply_fusion, f32[48,8]{1,0:T(8,128)S(1)} %get-tuple-element.7), kind=kLoop, calls=%fused_computation.16 | loop fusion | flops 4521984 | bytes 6687744 | tf_op jit(solution)/shard_map/reduce_sum | solution.py:103
  (15 shorter events, 0.1 us)
Async XLA Ops:
  7.2 362.9 %copy-start = (bf16[2048,64]{0,1:T(8,128)(2,1)S(1)}, bf16[2048,64]{0,1:T(8,128)(2,1)}, u32[]{:S(2)}) copy-start(bf16[2048,64]{0,1:T(8,128)(2,1)} %param.11) | copy-start | bytes 786436
  7.2 198.7 %all-gather.5.cloned.1.call-start = ((), (), s32[]{:S(2)}) async-start(), calls=%async_computation.5 | async-start | bytes 7077888 | tf_op jit(solution)/shard_map/all_gather | solution.py:76
  50.5 27.1 %all-to-all-start.1 = ((s32[32,1,24]{2,1,0:T(1,128)}), s32[32,1,24]{2,1,0:T(1,128)S(1)}, u32[]{:S(2)}, u32[]{:S(2)}) async-start(s32[32,1,24]{2,1,0:T(1,128)} %bitcast.50), calls=%async_computation.1 | async-start | bytes 32768 | tf_op jit(solution)/shard_map/all_to_all | solution.py:56
  77.6 95.2 %copy-start.2 = (bf16[2,96,2048]{2,1,0:T(8,128)(2,1)S(1)}, bf16[2,96,2048]{2,1,0:T(8,128)(2,1)}, u32[]{:S(2)}) copy-start(bf16[2,96,2048]{2,1,0:T(8,128)(2,1)} %param.17) | copy-start | bytes 2359300
  77.6 95.2 %all-to-all-start = ((bf16[32,24,4096]{2,1,0:T(8,128)(2,1)}), bf16[32,24,4096]{2,1,0:T(8,128)(2,1)}, u32[]{:S(2)}, u32[]{:S(2)}) async-start(bf16[32,24,4096]{2,1,0:T(8,128)(2,1)} %bitcast.134), calls=%async_computation | async-start | bytes 12582912 | tf_op jit(solution)/shard_map/all_to_all | solution.py:55
  85.2 127.1 %all-gather.3.cloned.1.call-start = ((), (), s32[]{:S(2)}) async-start(), calls=%async_computation.4 | async-start | bytes 7077888 | tf_op jit(solution)/shard_map/all_gather | solution.py:75
  176.2 150.0 %all-to-all-start.2 = ((bf16[8,2,96,2048]{3,2,1,0:T(8,128)(2,1)}), bf16[8,2,96,2048]{3,2,1,0:T(8,128)(2,1)}, u32[]{:S(2)}, u32[]{:S(2)}) async-start(bf16[8,2,96,2048]{3,2,1,0:T(8,128)(2,1)} %stack.6), calls=%async_computation.2 | async-start | bytes 12582912 | tf_op jit(solution)/shard_map/all_to_all | solution.py:78
  220.1 112.6 %copy-start.4 = (bf16[2,1,192,768]{3,2,1,0:T(8,128)(2,1)S(1)}, bf16[2,1,192,768]{3,2,1,0:T(8,128)(2,1)}, u32[]{:S(2)}) copy-start(bf16[2,1,192,768]{3,2,1,0:T(8,128)(2,1)} %get-tuple-element.9) | copy-start | bytes 1769476
  364.9 5.1 %copy-start.3 = (bf16[48,2048]{1,0:T(8,128)(2,1)S(1)}, bf16[48,2048]{1,0:T(8,128)(2,1)}, u32[]{:S(2)}) copy-start(bf16[48,2048]{1,0:T(8,128)(2,1)} %param.10) | copy-start | bytes 589828
  364.9 5.4 %copy-start.1 = (bf16[48,2048]{1,0:T(8,128)(2,1)S(1)}, bf16[48,2048]{1,0:T(8,128)(2,1)}, u32[]{:S(2)}) copy-start(bf16[48,2048]{1,0:T(8,128)(2,1)} %param.9) | copy-start | bytes 589828
  364.9 5.6 %copy-start.5 = (bf16[2048,64]{0,1:T(8,128)(2,1)S(1)}, bf16[2048,64]{0,1:T(8,128)(2,1)}, u32[]{:S(2)}) copy-start(bf16[2048,64]{0,1:T(8,128)(2,1)} %param.12) | copy-start | bytes 786436
  364.9 92.7 %all-to-all-start.3 = ((bf16[32,24,4096]{2,1,0:T(8,128)(2,1)}), bf16[32,24,4096]{2,1,0:T(8,128)(2,1)}, u32[]{:S(2)}, u32[]{:S(2)}) async-start(bf16[32,24,4096]{2,1,0:T(8,128)(2,1)} %reshape.209), calls=%async_computation.3 | async-start | bytes 12582912 | tf_op jit(solution)/shard_map/all_to_all | solution.py:89
Sparse Core Ops, SparseCore 0:
  9.8 77.3 all-gather.4
  89.0 76.0 all-gather.2
